TPU v7x, 32 devices: a whole 2x2x4 slice. The times are simulated.
32 devices in a mesh: dp: 8 (over z, y), rows: 4 (over x, core).
Axes of the slice: x: 2, y: 2, z: 4, core: 2. Of those that a mesh axis runs over, the one named last changes fastest.
Arguments:
- images: bfloat16 [8, 48, 64, 256], P('dp', 'rows'), may hold values from -6 to 6
- kernel: bfloat16 [3, 3, 256, 256], replicated, may hold values from -0.125 to 0.125
- cotangent: bfloat16 [8, 48, 64, 256], P('dp', 'rows'), may hold values from -6 to 6
Outputs:
- output_maps: bfloat16 [8, 48, 64, 256], P('dp', 'rows')
- grad_input: bfloat16 [8, 48, 64, 256], P('dp', 'rows')
- grad_kernel: float32 [3, 3, 256, 256], P(None, None, None, 'rows')
All inputs are finite; a program needn't handle non-finite values.
Results may differ from a plain program's by a relative error of at most 0.001.
Values may be sent and summed in bfloat16 or wider, within the bound.
A program may use at most 64 MiB of HBM per device.

v0:
```python
import jax
import jax.numpy as jnp
from jax import lax
from jax.sharding import PartitionSpec as P


def padded_2(x, sides, width):
    for axis, dim in sides:
        size, length = (lax.axis_size(axis), x.shape[dim])
        up = [(i, (i + 1) % size) for i in range(size - 1)]
        down = [(j, i) for i, j in up]
        last = lax.slice_in_dim(x, length - width, length, axis=dim)
        initial = lax.slice_in_dim(x, 0, width, axis=dim)
        before = lax.ppermute(last, axis, up)
        after = lax.ppermute(initial, axis, down)
        x = jnp.concatenate([before, x, after], axis=dim)
    return x


def conv_rows(inputs, weights):
    return lax.conv_general_dilated(
        inputs,
        weights,
        (1, 1),
        ((0, 0), (1, 1)),
        dimension_numbers=("NHWC", "HWIO", "NHWC"),
        preferred_element_type=jnp.float32,
    )


def shards(images, kernel, cotangent):
    rows_dev = images.shape[1]
    columns = images.shape[2]
    wide_images = padded_2(images, (("rows", 1),), 1)
    wide_grads = padded_2(cotangent, (("rows", 1),), 1)
    flipped = jnp.transpose(kernel[::-1, ::-1], (0, 1, 3, 2))
    output_maps = conv_rows(wide_images, kernel).astype(jnp.bfloat16)
    grad_input = conv_rows(wide_grads, flipped).astype(jnp.bfloat16)
    padded = jnp.pad(wide_images, ((0, 0), (0, 0), (1, 1), (0, 0)))
    tap_rows = []
    for tap_row in range(3):
        tap_line = []
        for tap_col in range(3):
            window = padded[:, tap_row : tap_row + rows_dev, tap_col : tap_col + columns]
            tap_line.append(
                jnp.einsum("bhwc,bhwd->cd", window, cotangent, preferred_element_type=jnp.float32)
            )
        tap_rows.append(jnp.stack(tap_line))
    local_terms = jnp.stack(tap_rows)
    groups = lax.axis_size("dp")
    row_share = lax.psum_scatter(local_terms, "rows", scatter_dimension=3, tiled=True)
    summed = lax.psum(row_share, "dp")
    batch_total = images.shape[0] * groups
    return (output_maps, grad_input, summed / float(batch_total))


def solution(mesh):
    return jax.shard_map(
        shards,
        mesh=mesh,
        in_specs=(P("dp", "rows", None, None), P(), P("dp", "rows", None, None)),
        out_specs=(
            P("dp", "rows", None, None),
            P("dp", "rows", None, None),
            P(None, None, None, "rows"),
        ),
        check_vma=False,
    )
```

profile of v0, /device:TPU:0, one launch (start us, length us, event | category | flops | bytes accessed | tf_op | source)
XLA Modules:
  0.0 180.4 jit_solution(7106152800115837669)
XLA Ops:
  7.2 0.9 fusion.67
  8.2 2.3 %collective-permute-start = (bf16[1,1,64,256]{3,2,1,0:T(8,128)(2,1)S(1)}, bf16[1,1,64,256]{3,2,1,0:T(8,128)(2,1)S(1)}, u32[]{:S(2)}, u32[]{:S(2)}) collective-permute-start(bf16[1,1,64,256]{3,2,1,0:T(8,128)(2,1)S(1)} %get-tuple-element.15), channel_id=1, source_target_pairs={{0,1},{1,2},{2,3},{4,5},{5,6},{6,7},{8,9},{9,10},{10,11},{12,13},{... | collective-permute-start | bytes 98312 | tf_op jit(solution)/shard_map/ppermute | solution.py:14
  10.5 1.3 collective-permute-start.1
  11.8 1.4 convolution_bitcast_fusion.4
  13.3 2.4 %collective-permute-done.1 = bf16[1,1,64,256]{3,2,1,0:T(8,128)(2,1)S(1)} collective-permute-done((bf16[1,1,64,256]{3,2,1,0:T(8,128)(2,1)S(1)}, bf16[1,1,64,256]{3,2,1,0:T(8,128)(2,1)S(1)}, u32[]{:S(2)}, u32[]{:S(2)}) %collective-permute-start.1) | collective-permute-done | bytes 32800 | tf_op jit(solution)/shard_map/ppermute | solution.py:15
  15.7 0.3 convolution_bitcast_fusion.3
  17.0 0.3 convolution_bitcast_fusion
  17.6 0.3 convolution_bitcast_fusion.1
  18.0 0.3 convolution_bitcast_fusion.7
  18.6 2.9 %copy.26 = f32[3,3,256,256]{2,1,0,3:T(4,128)} copy(f32[3,3,256,256]{3,2,1,0:T(8,128)S(1)} %pad_maximum_fusion) | data formatting | bytes 4718592 | tf_op jit(solution)/shard_map/stack | solution.py:49
  21.6 0.9 copy-done.2
  22.5 4.5 %collective-permute-start.2 = (bf16[1,1,64,256]{3,2,1,0:T(8,128)(2,1)S(1)}, bf16[1,1,64,256]{3,2,1,0:T(8,128)(2,1)S(1)}, u32[]{:S(2)}, u32[]{:S(2)}) collective-permute-start(bf16[1,1,64,256]{3,2,1,0:T(8,128)(2,1)S(1)} %get-tuple-element.12), channel_id=1, source_target_pairs={{0,1},{1,2},{2,3},{4,5},{5,6},{6,7},{8,9},{9,10},{10,11},{12,13},{... | collective-permute-start | bytes 98312 | tf_op jit(solution)/shard_map/ppermute | solution.py:14
  27.0 1.3 collective-permute-start.3
  28.3 0.6 dynamic-slice
  30.1 0.4 copy-done.7
  30.6 1.2 fusion
  31.9 61.2 %all-reduce.7.cloned.1.call-done = f32[3,3,256,256]{2,1,0,3:T(4,128)} async-done(((f32[3,3,256,256]{2,1,0,3:T(4,128)}), f32[3,3,256,256]{2,1,0,3:T(4,128)}) %all-reduce.7.cloned.1.call-update) | async-done | bytes 2359312
  93.1 2.2 %constant_dynamic-slice_fusion = f32[3,3,256,64]{2,1,0,3:T(4,128)} fusion(f32[3,3,256,256]{2,1,0,3:T(4,128)} %all-reduce.7.cloned.1.call-done, u32[]{:T(128)S(6)} %multiply.2), kind=kLoop, calls=%fused_computation.73 | loop fusion | bytes 1179652
  95.4 0.9 copy.27
  96.8 1.2 fusion.1
  98.2 0.9 copy.28
  99.0 72.3 %all-reduce.5.cloned.1.call-done = f32[3,3,256,64]{2,1,0,3:T(4,128)} async-done(((f32[3,3,256,64]{2,1,0,3:T(4,128)}), f32[3,3,256,64]{2,1,0,3:T(4,128)}) %all-reduce.5.cloned.1.call-update) | async-done | bytes 589840 | tf_op jit(solution)/shard_map/psum | solution.py:52
  171.3 1.3 broadcast_multiply_fusion
  172.6 0.9 copy.29
  (45 shorter events, 3.1 us)
Async XLA Ops:
  7.2 23.0 %copy-start = (bf16[3,3,256,256]{3,2,1,0:T(8,128)(2,1)S(1)}, bf16[3,3,256,256]{3,2,1,0:T(8,128)(2,1)}, u32[]{:S(2)}) copy-start(bf16[3,3,256,256]{3,2,1,0:T(8,128)(2,1)} %param.4) | copy-start | bytes 3538948
  7.2 6.1 %copy-start.3 = (bf16[1,12,64,256]{3,2,1,0:T(8,128)(2,1)S(1)}, bf16[1,12,64,256]{3,2,1,0:T(8,128)(2,1)}, u32[]{:S(2)}) copy-start(bf16[1,12,64,256]{3,2,1,0:T(8,128)(2,1)} %param.3) | copy-start | bytes 1179652
  7.2 8.5 %copy-start.1 = (bf16[1,12,64,256]{3,2,1,0:T(8,128)(2,1)S(1)}, bf16[1,12,64,256]{3,2,1,0:T(8,128)(2,1)}, u32[]{:S(2)}) copy-start(bf16[1,12,64,256]{3,2,1,0:T(8,128)(2,1)} %param.5) | copy-start | bytes 1179652
  7.2 85.9 %all-reduce.7.cloned.1.call-start = ((), (), s32[]{:S(2)}) async-start(), calls=%async_computation.1 | async-start | bytes 6291456
  8.2 5.1 %collective-permute-start = (bf16[1,1,64,256]{3,2,1,0:T(8,128)(2,1)S(1)}, bf16[1,1,64,256]{3,2,1,0:T(8,128)(2,1)S(1)}, u32[]{:S(2)}, u32[]{:S(2)}) collective-permute-start(bf16[1,1,64,256]{3,2,1,0:T(8,128)(2,1)S(1)} %get-tuple-element.15), channel_id=1, source_target_pairs={{0,1},{1,2},{2,3},{4,5},{5,6},{6,7},{8,9},{9,10},{10,11},{12,13},{... | collective-permute-start | bytes 98312 | tf_op jit(solution)/shard_map/ppermute | solution.py:14
  10.5 5.2 %collective-permute-start.1 = (bf16[1,1,64,256]{3,2,1,0:T(8,128)(2,1)S(1)}, bf16[1,1,64,256]{3,2,1,0:T(8,128)(2,1)S(1)}, u32[]{:S(2)}, u32[]{:S(2)}) collective-permute-start(bf16[1,1,64,256]{3,2,1,0:T(8,128)(2,1)S(1)} %get-tuple-element.14), channel_id=1, source_target_pairs={{1,0},{2,1},{3,2},{5,4},{6,5},{7,6},{9,8},{10,9},{11,10},{13,12},{... | collective-permute-start | bytes 98312 | tf_op jit(solution)/shard_map/ppermute | solution.py:15
  15.7 1.6 copy-start.4
  21.5 1.0 copy-start.2
  21.5 6.8 %copy-start.6 = (u32[32]{0:T(128)S(1)}, u32[32]{0:T(128)}, u32[]{:S(2)}) copy-start(u32[32]{0:T(128)} %constant.22) | copy-start | bytes 388
  21.5 8.1 %copy-start.5 = (bf16[1,14,64,256]{3,2,1,0:T(8,128)(2,1)S(1)}, bf16[1,14,64,256]{3,2,1,0:T(8,128)(2,1)}, u32[]{:S(2)}) copy-start(bf16[1,14,64,256]{3,2,1,0:T(8,128)(2,1)} %copy-done.4) | copy-start | bytes 1376260
  21.5 149.8 %all-reduce.5.cloned.1.call-start = ((), (), s32[]{:S(2)}) async-start(), calls=%async_computation | async-start | bytes 1572864 | tf_op jit(solution)/shard_map/psum | solution.py:52
  22.5 72.8 %collective-permute-start.2 = (bf16[1,1,64,256]{3,2,1,0:T(8,128)(2,1)S(1)}, bf16[1,1,64,256]{3,2,1,0:T(8,128)(2,1)S(1)}, u32[]{:S(2)}, u32[]{:S(2)}) collective-permute-start(bf16[1,1,64,256]{3,2,1,0:T(8,128)(2,1)S(1)} %get-tuple-element.12), channel_id=1, source_target_pairs={{0,1},{1,2},{2,3},{4,5},{5,6},{6,7},{8,9},{9,10},{10,11},{12,13},{... | collective-permute-start | bytes 98312 | tf_op jit(solution)/shard_map/ppermute | solution.py:14
  27.0 68.3 %collective-permute-start.3 = (bf16[1,1,64,256]{3,2,1,0:T(8,128)(2,1)S(1)}, bf16[1,1,64,256]{3,2,1,0:T(8,128)(2,1)S(1)}, u32[]{:S(2)}, u32[]{:S(2)}) collective-permute-start(bf16[1,1,64,256]{3,2,1,0:T(8,128)(2,1)S(1)} %get-tuple-element.13), channel_id=1, source_target_pairs={{1,0},{2,1},{3,2},{5,4},{6,5},{7,6},{9,8},{10,9},{11,10},{13,12},{... | collective-permute-start | bytes 98312 | tf_op jit(solution)/shard_map/ppermute | solution.py:15
  29.9 0.7 copy-start.7
Sparse Core Ops, SparseCore 0:
  21.6 71.3 all-reduce.6
  96.5 74.8 all-reduce.4
where the time goes:
time: 181 us; the launch traced here: 180 us
  waiting for transfers between devices  136 us (75%)
  between operations  15 us (8%)
  local copies, waits for them, and re-layouts  11.9 us (7%)
  starting transfers between devices  9.53 us (5%)
  matrix products  6.31 us (3%)
    psum x1, waiting for transfers between devices, shards(): summed = lax.psum(row_share, 'dp')  72.3 us
    unnamed x3, waiting for transfers between devices  61.2 us
    unnamed x25, local copies, waits for them, and re-layouts  7.31 us
    ppermute x2, starting transfers between devices, padded_2(): before = lax.ppermute(last, axis, up)  6.87 us
    dot_general x9, matrix products, shards(): jnp.einsum('bhwc,bhwd->cd', window, cotangent, preferred_element_type=jnp...  3.87 us
  transfers between devices with their start and end apart: 6, of which 3 were waited for; matrix products, arithmetic and copies ran while one was open for 5% of the time, Pallas kernels for 0%

commit v1 on v0

--- a/solution.py
+++ b/solution.py
@@ -2,6 +2,12 @@
 import jax.numpy as jnp
 from jax import lax
 from jax.sharding import PartitionSpec as P
+
+
+def summed_here(x, name):
+    pieces = lax.all_gather(x, name, axis=0, tiled=False)
+    summed = pieces.sum(axis=0)
+    return summed
 
 
 def padded_2(x, sides, width):
@@ -49,7 +55,7 @@
     local_terms = jnp.stack(tap_rows)
     groups = lax.axis_size("dp")
     row_share = lax.psum_scatter(local_terms, "rows", scatter_dimension=3, tiled=True)
-    summed = lax.psum(row_share, "dp")
+    summed = summed_here(row_share, "dp")
     batch_total = images.shape[0] * groups
     return (output_maps, grad_input, summed / float(batch_total))
 

time: 181 us -> 187 us (1.033)
  waiting for transfers between devices: 136 us -> 143 us
  starting transfers between devices: 9.53 us -> 6.63 us
    psum x1 -> x0, waiting for transfers between devices: 72.3 us -> none  [shards(): summed = lax.psum(row_share, 'dp')]
    all_gather x0 -> x1, waiting for transfers between devices: none -> 71.5 us  [summed_here(): pieces = lax.all_gather(x, name, axis=0, tiled=False)]
    unnamed x3, waiting for transfers between devices: 61.2 us -> 69.4 us
    ppermute x2, starting transfers between devices: 6.87 us -> 3.96 us  [padded_2(): before = lax.ppermute(last, axis, up)]
    reduce_sum x0 -> x1, other arithmetic: none -> 2.72 us  [summed_here(): summed = pieces.sum(axis=0)]
    unnamed x25 -> x26, local copies, waits for them, and re-layouts: 7.31 us -> 6.71 us
  transfers between devices with their start and end apart: 6 -> 6, of which waited for: 3 -> 3; matrix products, arithmetic and copies ran while one was open for 5% -> 4% of each run, Pallas kernels for 0% -> 0%
where the time goes in v1:
time: 187 us
  waiting for transfers between devices  143 us (76%)
  between operations  15 us (8%)
  local copies, waits for them, and re-layouts  12.2 us (7%)
  starting transfers between devices  6.63 us (4%)
  matrix products  6.31 us (3%)
  other arithmetic  3.18 us (2%)
    all_gather x1, waiting for transfers between devices, summed_here(): pieces = lax.all_gather(x, name, axis=0, tiled=False)  71.5 us
    unnamed x3, waiting for transfers between devices  69.4 us
    unnamed x26, local copies, waits for them, and re-layouts  6.71 us
    ppermute x2, starting transfers between devices, padded_2(): before = lax.ppermute(last, axis, up)  3.96 us
    dot_general x9, matrix products, shards(): jnp.einsum('bhwc,bhwd->cd', window, cotangent, preferred_element_type=jnp...  3.87 us
  transfers between devices with their start and end apart: 6, of which 3 were waited for; matrix products, arithmetic and copies ran while one was open for 4% of the time, Pallas kernels for 0%

profile of v1, /device:TPU:0, one launch (start us, length us, event | category | flops | bytes accessed | tf_op | source)
XLA Modules:
  0.0 186.7 jit_solution(199234966947611152)
XLA Ops:
  7.2 0.9 fusion.67
  8.2 2.3 %collective-permute-start = (bf16[1,1,64,256]{3,2,1,0:T(8,128)(2,1)S(1)}, bf16[1,1,64,256]{3,2,1,0:T(8,128)(2,1)S(1)}, u32[]{:S(2)}, u32[]{:S(2)}) collective-permute-start(bf16[1,1,64,256]{3,2,1,0:T(8,128)(2,1)S(1)} %get-tuple-element.12), channel_id=1, source_target_pairs={{0,1},{1,2},{2,3},{4,5},{5,6},{6,7},{8,9},{9,10},{10,11},{12,13},{... | collective-permute-start | bytes 98312 | tf_op jit(solution)/shard_map/ppermute | solution.py:20
  10.5 1.3 collective-permute-start.1
  11.8 1.4 convolution_bitcast_fusion.4
  13.3 2.4 %collective-permute-done.1 = bf16[1,1,64,256]{3,2,1,0:T(8,128)(2,1)S(1)} collective-permute-done((bf16[1,1,64,256]{3,2,1,0:T(8,128)(2,1)S(1)}, bf16[1,1,64,256]{3,2,1,0:T(8,128)(2,1)S(1)}, u32[]{:S(2)}, u32[]{:S(2)}) %collective-permute-start.1) | collective-permute-done | bytes 32800 | tf_op jit(solution)/shard_map/ppermute | solution.py:21
  17.6 0.3 convolution_bitcast_fusion.1
  18.0 0.3 convolution_bitcast_fusion.7
  18.6 2.9 %copy.24 = f32[3,3,256,256]{2,1,0,3:T(4,128)} copy(f32[3,3,256,256]{3,2,1,0:T(8,128)S(1)} %pad_maximum_fusion) | data formatting | bytes 4718592 | tf_op jit(solution)/shard_map/stack | solution.py:55
  21.6 0.6 copy-done.6
  22.1 0.6 dynamic-slice
  23.4 69.3 %all-reduce.4.cloned.1.call-done = f32[3,3,256,256]{2,1,0,3:T(4,128)} async-done(((f32[3,3,256,256]{2,1,0,3:T(4,128)}), f32[3,3,256,256]{2,1,0,3:T(4,128)}) %all-reduce.4.cloned.1.call-update) | async-done | bytes 2359312
  92.7 1.3 constant_dynamic-slice_fusion
  94.0 0.9 copy.25
  95.0 1.6 collective-permute-start.2
  96.6 1.3 collective-permute-start.3
  98.5 0.4 copy-done.7
  98.9 1.2 fusion
  100.2 0.9 copy.27
  101.7 1.2 fusion.1
  103.1 0.9 copy.28
  104.0 71.5 %all-gather.3.cloned.1.call-done = f32[24,3,256,64]{2,3,1,0:T(8,128)} async-done(((f32[3,3,256,64]{2,3,1,0:T(8,128)}), f32[24,3,256,64]{2,3,1,0:T(8,128)}) %all-gather.3.cloned.1.call-update) | async-done | bytes 4718608 | tf_op jit(solution)/shard_map/all_gather | solution.py:8
  175.5 2.7 %reduce_sum.9 = f32[3,3,256,64]{2,3,1,0:T(8,128)S(1)} reduce(f32[8,3,3,256,64]{3,4,2,1,0:T(8,128)} %bitcast.100, f32[]{:T(128)} %constant.6.clone.1), dimensions={0}, to_apply=%region_1.2 | reduce | flops 1032192 | bytes 5308420 | tf_op jit(solution)/shard_map/reduce_sum | solution.py:9
  178.2 0.4 copy.30
  178.7 1.2 copy.29
  (48 shorter events, 3.8 us)
Async XLA Ops:
  7.2 91.3 %copy-start = (bf16[3,3,256,256]{3,2,1,0:T(8,128)(2,1)S(1)}, bf16[3,3,256,256]{3,2,1,0:T(8,128)(2,1)}, u32[]{:S(2)}) copy-start(bf16[3,3,256,256]{3,2,1,0:T(8,128)(2,1)} %param.4) | copy-start | bytes 3538948
  7.2 6.1 %copy-start.3 = (bf16[1,12,64,256]{3,2,1,0:T(8,128)(2,1)S(1)}, bf16[1,12,64,256]{3,2,1,0:T(8,128)(2,1)}, u32[]{:S(2)}) copy-start(bf16[1,12,64,256]{3,2,1,0:T(8,128)(2,1)} %param.3) | copy-start | bytes 1179652
  7.2 8.5 %copy-start.1 = (bf16[1,12,64,256]{3,2,1,0:T(8,128)(2,1)S(1)}, bf16[1,12,64,256]{3,2,1,0:T(8,128)(2,1)}, u32[]{:S(2)}) copy-start(bf16[1,12,64,256]{3,2,1,0:T(8,128)(2,1)} %param.5) | copy-start | bytes 1179652
  7.2 85.5 %all-reduce.4.cloned.1.call-start = ((), (), s32[]{:S(2)}) async-start(), calls=%async_computation.1 | async-start | bytes 6291456
  8.2 5.1 %collective-permute-start = (bf16[1,1,64,256]{3,2,1,0:T(8,128)(2,1)S(1)}, bf16[1,1,64,256]{3,2,1,0:T(8,128)(2,1)S(1)}, u32[]{:S(2)}, u32[]{:S(2)}) collective-permute-start(bf16[1,1,64,256]{3,2,1,0:T(8,128)(2,1)S(1)} %get-tuple-element.12), channel_id=1, source_target_pairs={{0,1},{1,2},{2,3},{4,5},{5,6},{6,7},{8,9},{9,10},{10,11},{12,13},{... | collective-permute-start | bytes 98312 | tf_op jit(solution)/shard_map/ppermute | solution.py:20
  10.5 5.2 %collective-permute-start.1 = (bf16[1,1,64,256]{3,2,1,0:T(8,128)(2,1)S(1)}, bf16[1,1,64,256]{3,2,1,0:T(8,128)(2,1)S(1)}, u32[]{:S(2)}, u32[]{:S(2)}) collective-permute-start(bf16[1,1,64,256]{3,2,1,0:T(8,128)(2,1)S(1)} %get-tuple-element.11), channel_id=1, source_target_pairs={{1,0},{2,1},{3,2},{5,4},{6,5},{7,6},{9,8},{10,9},{11,10},{13,12},{... | collective-permute-start | bytes 98312 | tf_op jit(solution)/shard_map/ppermute | solution.py:21
  15.7 1.6 copy-start.4
  21.5 0.7 copy-start.6
  21.5 154.0 %all-gather.3.cloned.1.call-start = ((), (), s32[]{:S(2)}) async-start(), calls=%async_computation | async-start | bytes 5308416 | tf_op jit(solution)/shard_map/all_gather | solution.py:8
  94.0 1.0 copy-start.2
  94.0 3.9 %copy-start.5 = (bf16[1,14,64,256]{3,2,1,0:T(8,128)(2,1)S(1)}, bf16[1,14,64,256]{3,2,1,0:T(8,128)(2,1)}, u32[]{:S(2)}) copy-start(bf16[1,14,64,256]{3,2,1,0:T(8,128)(2,1)} %copy-done.4) | copy-start | bytes 1376260
  95.0 6.1 %collective-permute-start.2 = (bf16[1,1,64,256]{3,2,1,0:T(8,128)(2,1)S(1)}, bf16[1,1,64,256]{3,2,1,0:T(8,128)(2,1)S(1)}, u32[]{:S(2)}, u32[]{:S(2)}) collective-permute-start(bf16[1,1,64,256]{3,2,1,0:T(8,128)(2,1)S(1)} %get-tuple-element.9), channel_id=1, source_target_pairs={{0,1},{1,2},{2,3},{4,5},{5,6},{6,7},{8,9},{9,10},{10,11},{12,13},{... | collective-permute-start | bytes 98312 | tf_op jit(solution)/shard_map/ppermute | solution.py:20
  96.6 4.5 %collective-permute-start.3 = (bf16[1,1,64,256]{3,2,1,0:T(8,128)(2,1)S(1)}, bf16[1,1,64,256]{3,2,1,0:T(8,128)(2,1)S(1)}, u32[]{:S(2)}, u32[]{:S(2)}) collective-permute-start(bf16[1,1,64,256]{3,2,1,0:T(8,128)(2,1)S(1)} %get-tuple-element.10), channel_id=1, source_target_pairs={{1,0},{2,1},{3,2},{5,4},{6,5},{7,6},{9,8},{10,9},{11,10},{13,12},{... | collective-permute-start | bytes 98312 | tf_op jit(solution)/shard_map/ppermute | solution.py:21
  98.2 0.7 copy-start.7
Sparse Core Ops, SparseCore 0:
  21.6 71.0 all-reduce.3
  95.5 79.9 all-gather.2
